TPU v7x, 32 devices: a whole 2x2x4 slice. The times are simulated.
32 devices in a mesh: tm: 8 (over z, x), panel: 4 (over y, core).
Axes of the slice: x: 2, y: 2, z: 4, core: 2. Of those that a mesh axis runs over, the one named last changes fastest.
Arguments:
- spins: int32 [8, 1152], P('tm'), may hold values from -1 to 1, as said below
- neighbours: int32 [1152, 4], replicated, may hold values from 0 to 1151, as said below
- start: float32 [9216, 1152], P(('tm', 'panel')), may hold values from -6 to 6
Outputs:
- panels: float32 [9216, 1152], P(('tm', 'panel'))
- growth: float32 [9216], P(('tm', 'panel'))
Inputs may be any that keep to these rules, and one draw needn't show every extreme that they name: `spins`: each entry is -1 or +1. The nearest neighbours of a periodic (24) x 48 square lattice whose sites carry a random labelling; the table is symmetric.
All inputs are finite; a program needn't handle non-finite values.
Results may differ from a plain program's by a relative error of at most 0.0092.
Values may be sent and summed in bfloat16 or wider, within the bound.
A program may use at most 64 MiB of HBM per device.

v0:
```python
import jax
import jax.numpy as jnp
from jax import lax
from jax.sharding import PartitionSpec as P

STEPS = 4


DTAU = 0.0625
LAMBDA = 0.5
EPS = 1e-06


def from_behind(value, axis, by):
    length = lax.axis_size(axis)
    return lax.ppermute(value, axis, [(i, (i + by) % length) for i in range(length)])


def adjacency(neighbours, rows, labels):
    picked = neighbours[rows]
    total = jnp.zeros((rows.shape[0], labels.shape[0]), jnp.float32)
    for k in range(4):
        total = total + (picked[:, k][:, None] == labels[None, :]).astype(jnp.float32)
    return total


def propagator(neighbours, rows, labels):
    krows = adjacency(neighbours, rows, labels)
    kfull = adjacency(neighbours, labels, labels).astype(jnp.bfloat16)
    ksq = jnp.dot(krows.astype(jnp.bfloat16), kfull, preferred_element_type=jnp.float32)
    eye_rows = (rows[:, None] == labels[None, :]).astype(jnp.float32)
    return (eye_rows + DTAU * krows + 0.5 * DTAU * DTAU * ksq).astype(jnp.bfloat16)


def weights_of(spin_row):
    return jnp.exp(LAMBDA * spin_row.astype(jnp.float32))


def shards(spins, neighbours, start):
    sites = neighbours.shape[0]
    width = start.shape[0]
    labels = jnp.arange(sites, dtype=jnp.int32)
    offset = lax.axis_index("panel") * width
    own_rows = offset + jnp.arange(width, dtype=jnp.int32)
    factor = weights_of(spins[0])
    hop_part = propagator(neighbours, own_rows, labels)
    hop = lax.all_gather(hop_part, "panel", axis=0, tiled=True)

    def advance(panel_in, weights):
        return (
            jnp.dot(panel_in, hop, preferred_element_type=jnp.float32) * weights[None, :]
        ).astype(jnp.bfloat16)

    single = (hop_part.astype(jnp.float32) * factor[None, :]).astype(jnp.bfloat16)
    earlier = from_behind(single, "tm", 1)
    pair = advance(earlier, factor)
    triple = advance(from_behind(pair, "tm", 1), factor)
    block = advance(from_behind(triple, "tm", 1), factor)
    full_block = lax.all_gather(block, "panel", axis=0, tiled=True)
    sign = jnp.where(lax.axis_index("tm") < 4, -1.0, 1.0).astype(jnp.float32)
    current = start
    logsum = jnp.zeros((width,), jnp.float32)
    for step in range(STEPS):
        incoming = from_behind(current.astype(jnp.bfloat16), "tm", 4)
        image = jnp.dot(incoming, full_block, preferred_element_type=jnp.float32) * sign
        rms = jnp.sqrt(jnp.mean(image * image, axis=1) + EPS)
        current = image / rms[:, None]
        logsum = logsum + jnp.log(rms)
    return (current, logsum / (4.0 * STEPS))


def solution(mesh):
    return jax.shard_map(
        shards,
        mesh=mesh,
        in_specs=(P("tm", None), P(), P(("tm", "panel"), None)),
        out_specs=(P(("tm", "panel"), None), P(("tm", "panel"))),
        check_vma=False,
    )
```

profile of v0, /device:TPU:0, one launch (start us, length us, event | category | flops | bytes accessed | tf_op | source)
XLA Modules:
  0.0 229.4 jit_solution(12646457638772280125)
XLA Ops:
  7.2 0.0 all-gather.3.cloned.1.call-start
  7.3 1.0 copy.7
  8.2 1.1 gather_fusion
  9.3 0.4 slice_reduce_fusion.7
  9.7 2.4 %gather_fusion.1 = s32[1152,4]{1,0:T(8,128)S(1)} fusion(s32[1152,4]{1,0:T(8,128)S(1)} %copy.7, s32[2048]{0:T(1024)S(1)} %pad_clamp_fusion), kind=kCustom, calls=%fused_computation.1 | custom fusion | bytes 41472 | tf_op jit(solution)/shard_map/gather | solution.py:20
  12.2 0.0 copy-start.1
  12.2 1.2 slice_reduce_fusion.3
  13.4 0.0 copy-done.1
  13.4 5.4 %multiply_convert_fusion = (bf16[288,1152]{1,0:T(8,128)(2,1)S(1)}, bf16[288,1152]{1,0:T(8,128)(2,1)}) fusion(f32[1152]{0:T(1024)S(1)} %exponential_reduce_fusion, s32[1152]{0:T(1024)S(1)} %get-tuple-element.5, s32[1152]{0:T(1024)S(1)} %get-tuple-element.3, s32[1152]{0:T(1024)S(1)} %get-tuple-element.4, s32[1152]{0:T(1024)S(1)} %get-tuple-element.2, ...), kind=kOutput, calls=%fused_computation.31 | convolution fusion | flops 791285760 | bytes 1355904 | tf_op jit(solution)/shard_map/dot_general | solution.py:30
  18.8 0.0 all-gather.3.cloned.1.call-update
  18.8 0.0 all-gather.5.cloned.1.call-start
  18.9 3.0 %collective-permute-start = (bf16[288,1152]{1,0:T(8,128)(2,1)S(1)}, bf16[288,1152]{1,0:T(8,128)(2,1)S(1)}, u32[]{:S(2)}, u32[]{:S(2)}) collective-permute-start(bf16[288,1152]{1,0:T(8,128)(2,1)S(1)} %get-tuple-element.12), channel_id=1, source_target_pairs={{0,4},{4,8},{8,12},{12,16},{16,20},{20,24},{24,28},{28,0},{1,5},{5... | collective-permute-start | bytes 1990664 | tf_op jit(solution)/shard_map/ppermute | solution.py:16
  21.9 17.9 %collective-permute-done = bf16[288,1152]{1,0:T(8,128)(2,1)S(1)} collective-permute-done((bf16[288,1152]{1,0:T(8,128)(2,1)S(1)}, bf16[288,1152]{1,0:T(8,128)(2,1)S(1)}, u32[]{:S(2)}, u32[]{:S(2)}) %collective-permute-start) | collective-permute-done | bytes 663584 | tf_op jit(solution)/shard_map/ppermute | solution.py:16
  39.8 7.6 %all-gather.3.cloned.1.call-done = bf16[1152,1152]{1,0:T(8,128)(2,1)} async-done(((bf16[288,1152]{1,0:T(8,128)(2,1)}), bf16[1152,1152]{1,0:T(8,128)(2,1)}) %all-gather.3.cloned.1.call-update) | async-done | bytes 2654224 | tf_op jit(solution)/shard_map/all_gather | solution.py:47
  47.4 0.0 copy-start.3
  47.4 3.0 %fusion.6 = bf16[288,1152]{1,0:T(8,128)(2,1)S(1)} fusion(bf16[288,1152]{1,0:T(8,128)(2,1)S(1)} %collective-permute-done, bf16[1152,1152]{1,0:T(8,128)(2,1)} %all-gather.3.cloned.1.call-done, f32[1152]{0:T(1024)S(1)} %exponential_reduce_fusion), kind=kOutput, calls=%fused_computation.21 | convolution fusion | flops 765075456 | bytes 3985920 | tf_op jit(solution)/shard_map/dot_general | solution.py:51
  50.5 1.5 collective-permute-start.1
  52.0 18.3 %collective-permute-done.1 = bf16[288,1152]{1,0:T(8,128)(2,1)S(1)} collective-permute-done((bf16[288,1152]{1,0:T(8,128)(2,1)S(1)}, bf16[288,1152]{1,0:T(8,128)(2,1)S(1)}, u32[]{:S(2)}, u32[]{:S(2)}) %collective-permute-start.1) | collective-permute-done | bytes 663584 | tf_op jit(solution)/shard_map/ppermute | solution.py:16
  70.3 0.0 copy-done.3
  70.3 1.1 fusion.7
  71.4 0.2 collective-permute-start.2
  71.6 18.9 %collective-permute-done.2 = bf16[288,1152]{1,0:T(8,128)(2,1)S(1)} collective-permute-done((bf16[288,1152]{1,0:T(8,128)(2,1)S(1)}, bf16[288,1152]{1,0:T(8,128)(2,1)S(1)}, u32[]{:S(2)}, u32[]{:S(2)}) %collective-permute-start.2) | collective-permute-done | bytes 663584 | tf_op jit(solution)/shard_map/ppermute | solution.py:16
  90.5 0.0 copy-start
  90.5 1.9 fusion.8
  92.5 0.0 all-gather.5.cloned.1.call-update
  92.5 0.0 copy-done
  92.5 0.1 convert_element_type.88
  92.6 0.1 collective-permute-start.3
  92.7 27.7 %collective-permute-done.3 = bf16[288,1152]{1,0:T(8,128)(2,1)S(1)} collective-permute-done((bf16[288,1152]{1,0:T(8,128)(2,1)S(1)}, bf16[288,1152]{1,0:T(8,128)(2,1)S(1)}, u32[]{:S(2)}, u32[]{:S(2)}) %collective-permute-start.3) | collective-permute-done | bytes 663584 | tf_op jit(solution)/shard_map/ppermute | solution.py:16
  120.4 0.0 all-gather.5.cloned.1.call-done
  120.4 0.0 copy-start.2
  120.4 3.1 %multiply_reduce_fusion.3 = (f32[288]{0:T(512)S(1)}, f32[1152,288]{0,1:T(8,128)S(1)}) fusion(f32[]{:T(128)S(6)} %select_n.16, bf16[288,1152]{1,0:T(8,128)(2,1)S(1)} %collective-permute-done.3, bf16[1152,1152]{1,0:T(8,128)(2,1)} %all-gather.5.cloned.1.call-done), kind=kOutput, calls=%fused_computation.30 | convolution fusion | flops 765406976 | bytes 4646020 | tf_op jit(solution)/shard_map/dot_general | solution.py:65
  123.6 0.2 fusion.15
  123.7 0.1 collective-permute-start.4
  123.8 30.2 %collective-permute-done.4 = bf16[288,1152]{1,0:T(8,128)(2,1)S(1)} collective-permute-done((bf16[288,1152]{1,0:T(8,128)(2,1)S(1)}, bf16[288,1152]{1,0:T(8,128)(2,1)S(1)}, u32[]{:S(2)}, u32[]{:S(2)}) %collective-permute-start.4) | collective-permute-done | bytes 663584 | tf_op jit(solution)/shard_map/ppermute | solution.py:16
  154.0 0.0 copy-done.2
  154.0 1.3 multiply_reduce_fusion.2
  155.3 0.2 divide_convert_fusion.1
  155.5 0.1 collective-permute-start.5
  155.5 31.6 %collective-permute-done.5 = bf16[288,1152]{1,0:T(8,128)(2,1)S(1)} collective-permute-done((bf16[288,1152]{1,0:T(8,128)(2,1)S(1)}, bf16[288,1152]{1,0:T(8,128)(2,1)S(1)}, u32[]{:S(2)}, u32[]{:S(2)}) %collective-permute-start.5) | collective-permute-done | bytes 663584 | tf_op jit(solution)/shard_map/ppermute | solution.py:16
  187.1 1.3 multiply_reduce_fusion.1
  188.4 0.2 divide_convert_fusion
  188.6 0.1 collective-permute-start.6
  188.6 30.8 %collective-permute-done.6 = bf16[288,1152]{1,0:T(8,128)(2,1)S(1)} collective-permute-done((bf16[288,1152]{1,0:T(8,128)(2,1)S(1)}, bf16[288,1152]{1,0:T(8,128)(2,1)S(1)}, u32[]{:S(2)}, u32[]{:S(2)}) %collective-permute-start.6) | collective-permute-done | bytes 663584 | tf_op jit(solution)/shard_map/ppermute | solution.py:16
  219.5 1.2 multiply_reduce_fusion
  220.7 0.6 add_multiply_fusion
  221.3 1.2 broadcast_divide_fusion
  (9 shorter events, 0.1 us)
Async XLA Ops:
  7.2 40.3 %all-gather.3.cloned.1.call-start = ((), (), s32[]{:S(2)}) async-start(), calls=%async_computation | async-start | bytes 3317760 | tf_op jit(solution)/shard_map/all_gather | solution.py:47
  12.2 1.2 copy-start.1
  18.8 101.6 %all-gather.5.cloned.1.call-start = ((), (), s32[]{:S(2)}) async-start(), calls=%async_computation.1 | async-start | bytes 3317760 | tf_op jit(solution)/shard_map/all_gather | solution.py:59
  18.9 20.9 %collective-permute-start = (bf16[288,1152]{1,0:T(8,128)(2,1)S(1)}, bf16[288,1152]{1,0:T(8,128)(2,1)S(1)}, u32[]{:S(2)}, u32[]{:S(2)}) collective-permute-start(bf16[288,1152]{1,0:T(8,128)(2,1)S(1)} %get-tuple-element.12), channel_id=1, source_target_pairs={{0,4},{4,8},{8,12},{12,16},{16,20},{20,24},{24,28},{28,0},{1,5},{5... | collective-permute-start | bytes 1990664 | tf_op jit(solution)/shard_map/ppermute | solution.py:16
  47.4 22.8 %copy-start.3 = (bf16[1152,1152]{1,0:T(8,128)(2,1)S(1)}, bf16[1152,1152]{1,0:T(8,128)(2,1)}, u32[]{:S(2)}) copy-start(bf16[1152,1152]{1,0:T(8,128)(2,1)} %all-gather.3.cloned.1.call-done) | copy-start | bytes 7962628
  50.5 19.8 %collective-permute-start.1 = (bf16[288,1152]{1,0:T(8,128)(2,1)S(1)}, bf16[288,1152]{1,0:T(8,128)(2,1)S(1)}, u32[]{:S(2)}, u32[]{:S(2)}) collective-permute-start(bf16[288,1152]{1,0:T(8,128)(2,1)S(1)} %fusion.6), channel_id=1, source_target_pairs={{0,4},{4,8},{8,12},{12,16},{16,20},{20,24},{24,28},{28,0},{1,5},{5... | collective-permute-start | bytes 1990664 | tf_op jit(solution)/shard_map/ppermute | solution.py:16
  71.4 19.2 %collective-permute-start.2 = (bf16[288,1152]{1,0:T(8,128)(2,1)S(1)}, bf16[288,1152]{1,0:T(8,128)(2,1)S(1)}, u32[]{:S(2)}, u32[]{:S(2)}) collective-permute-start(bf16[288,1152]{1,0:T(8,128)(2,1)S(1)} %fusion.7), channel_id=1, source_target_pairs={{0,4},{4,8},{8,12},{12,16},{16,20},{20,24},{24,28},{28,0},{1,5},{5... | collective-permute-start | bytes 1990664 | tf_op jit(solution)/shard_map/ppermute | solution.py:16
  90.5 2.0 copy-start
  92.6 27.8 %collective-permute-start.3 = (bf16[288,1152]{1,0:T(8,128)(2,1)S(1)}, bf16[288,1152]{1,0:T(8,128)(2,1)S(1)}, u32[]{:S(2)}, u32[]{:S(2)}) collective-permute-start(bf16[288,1152]{1,0:T(8,128)(2,1)S(1)} %convert_element_type.88), channel_id=1, source_target_pairs={{0,16},{4,20},{8,24},{12,28},{16,0},{20,4},{24,8},{28,12},{1,17},{... | collective-permute-start | bytes 1990664 | tf_op jit(solution)/shard_map/ppermute | solution.py:16
  120.4 33.6 %copy-start.2 = (bf16[1152,1152]{1,0:T(8,128)(2,1)S(1)}, bf16[1152,1152]{1,0:T(8,128)(2,1)}, u32[]{:S(2)}) copy-start(bf16[1152,1152]{1,0:T(8,128)(2,1)} %all-gather.5.cloned.1.call-done) | copy-start | bytes 7962628
  123.7 30.3 %collective-permute-start.4 = (bf16[288,1152]{1,0:T(8,128)(2,1)S(1)}, bf16[288,1152]{1,0:T(8,128)(2,1)S(1)}, u32[]{:S(2)}, u32[]{:S(2)}) collective-permute-start(bf16[288,1152]{1,0:T(8,128)(2,1)S(1)} %fusion.15), channel_id=1, source_target_pairs={{0,16},{4,20},{8,24},{12,28},{16,0},{20,4},{24,8},{28,12},{1,17},{... | collective-permute-start | bytes 1990664 | tf_op jit(solution)/shard_map/ppermute | solution.py:16
  155.5 31.7 %collective-permute-start.5 = (bf16[288,1152]{1,0:T(8,128)(2,1)S(1)}, bf16[288,1152]{1,0:T(8,128)(2,1)S(1)}, u32[]{:S(2)}, u32[]{:S(2)}) collective-permute-start(bf16[288,1152]{1,0:T(8,128)(2,1)S(1)} %divide_convert_fusion.1), channel_id=1, source_target_pairs={{0,16},{4,20},{8,24},{12,28},{16,0},{20,4},{24,8},{28,12},{1,17},{... | collective-permute-start | bytes 1990664 | tf_op jit(solution)/shard_map/ppermute | solution.py:16
  188.6 30.9 %collective-permute-start.6 = (bf16[288,1152]{1,0:T(8,128)(2,1)S(1)}, bf16[288,1152]{1,0:T(8,128)(2,1)S(1)}, u32[]{:S(2)}, u32[]{:S(2)}) collective-permute-start(bf16[288,1152]{1,0:T(8,128)(2,1)S(1)} %divide_convert_fusion), channel_id=1, source_target_pairs={{0,16},{4,20},{8,24},{12,28},{16,0},{20,4},{24,8},{28,12},{1,17},{... | collective-permute-start | bytes 1990664 | tf_op jit(solution)/shard_map/ppermute | solution.py:16
Sparse Core Ops, SparseCore 0:
  19.0 28.4 all-gather.2
  92.6 21.8 all-gather.4
where the time goes:
time: 230 us; the launch traced here: 229 us
  waiting for transfers between devices  183 us (80%)
  matrix products  18.3 us (8%)
  between operations  14.2 us (6%)
  local copies, waits for them, and re-layouts  6.07 us (3%)
  starting transfers between devices  5.12 us (2%)
  other arithmetic  2.51 us (1%)
    ppermute x7, waiting for transfers between devices, from_behind(): lax.ppermute(value, axis, [(i, (i + by) % length) for i in range(length)])  175 us
    all_gather x1, waiting for transfers between devices, shards(): hop = lax.all_gather(hop_part, 'panel', axis=0, tiled=True)  7.61 us
    dot_general x4, matrix products, shards(): jnp.dot(incoming, full_block, preferred_element_type=jnp.float32) * sign  6.86 us
    dot_general x3, matrix products, advance(): jnp.dot(panel_in, hop, preferred_element_type=jnp.float32)  6.06 us
    dot_general x1, matrix products, propagator(): jnp.dot(krows.astype(jnp.bfloat16), kfull, preferred_element_type=jnp.flo...  5.4 us
    ppermute x7, starting transfers between devices, from_behind(): lax.ppermute(value, axis, [(i, (i + by) % length) for i in range(length)])  5.04 us
  transfers between devices with their start and end apart: 9, of which 8 were waited for; matrix products, arithmetic and copies ran while one was open for 0% of the time, Pallas kernels for 0%

commit v1 on v0

v1 whole, which is shorter than its diff:
```python
import functools

import jax
import jax.numpy as jnp
from jax import lax
from jax.experimental import pallas as pl
from jax.experimental.pallas import tpu as pltpu
from jax.sharding import PartitionSpec as P

STEPS = 4
SPAN = 4
DTAU = 0.0625
LAMBDA = 0.5
EPS = 1e-06
TILE = 256
MESH = pl.DeviceIdType.MESH


def column_tiles(sites):
    return [(at, min(TILE, sites - at)) for at in range(0, sites, TILE)]


def kernel(
    slices, spins_ref, table_ref, start_ref, panels_ref, growth_ref,
    spins_all, factors, bonds, bonds8, rest, now, held, squares, logs, landed, scale_row,
    start_sem, spin_send, spin_recv, log_send, log_recv,
):
    rows, sites = now.shape
    hops = STEPS * SPAN
    tiles = column_tiles(sites)
    me = lax.axis_index("tm")

    def at(offset):
        return {"tm": lax.rem(me + (offset % slices), slices)}

    spin_reach = min(hops, slices)
    log_reach = [SPAN * (STEPS - 1 - s) % slices for s in range(STEPS)]
    log_dist = sorted({d for d in log_reach if d != 0})

    fetch = pltpu.make_async_copy(start_ref, now, start_sem)
    fetch.start()

    targets = set(range(1, spin_reach)) | {slices - d for d in log_dist}
    greeted = sorted(targets | {slices - d for d in targets})
    barrier = pltpu.get_barrier_semaphore()
    for offset in greeted:
        pl.semaphore_signal(barrier, inc=1, device_id=at(offset), device_id_type=MESH)
    spins_all[0] = spins_ref[...]

    chunk = rows // 3

    def build(c, carry):
        first = pl.multiple_of(c * chunk, chunk)
        label = lax.broadcasted_iota(jnp.int32, (chunk, sites), 0) + first
        hit = table_ref[0:1, :] == label
        for k in range(1, 4):
            hit = hit | (table_ref[k:k + 1, :] == label)
        value = jnp.where(hit, DTAU, 0.0)
        bonds[pl.ds(first, chunk), :] = value.astype(jnp.bfloat16)
        bonds8[pl.ds(first, chunk), :] = value.astype(bonds8.dtype)
        return carry

    lax.fori_loop(0, sites // chunk, build, 0)

    pl.semaphore_wait(barrier, len(greeted))
    sends = []
    for d in range(1, spin_reach):
        copy = pltpu.make_async_remote_copy(
            src_ref=spins_all.at[0], dst_ref=spins_all.at[d],
            send_sem=spin_send.at[d], recv_sem=spin_recv.at[d],
            device_id=at(d), device_id_type=MESH,
        )
        copy.start()
        sends.append(copy)

    def square(c, carry):
        first = pl.multiple_of(c * rows, rows)
        block = pl.ds(first, rows)
        for lo, width in tiles:
            twice = jnp.dot(bonds8[block, :], bonds8[:, lo:lo + width], preferred_element_type=jnp.float32)
            one = bonds[block, lo:lo + width].astype(jnp.float32)
            rest[block, lo:lo + width] = (one + 0.5 * twice).astype(jnp.bfloat16)
        return carry

    lax.fori_loop(0, sites // rows, square, 0)

    fetch.wait()
    held[0] = now[...].astype(jnp.bfloat16)
    now[...] = held[0].astype(jnp.float32)

    for copy in sends:
        copy.wait()
    factors[...] = jnp.exp(LAMBDA * spins_all[...].astype(jnp.float32))

    scale_row[...] = jnp.ones_like(scale_row)
    logs[...] = jnp.zeros_like(logs)
    ones = jnp.ones((8, 128), jnp.float32)

    def log_copy(i):
        return pltpu.make_async_remote_copy(
            src_ref=logs.at[1 + i], dst_ref=landed.at[i],
            send_sem=log_send.at[i], recv_sem=log_recv.at[i],
            device_id=at(slices - log_dist[i]), device_id_type=MESH,
        )

    def step(s, carry):
        for a in range(SPAN):
            behind = lax.rem(hops - 1 - SPAN * s - a, slices)
            factor = factors.at[behind]
            last = a == SPAN - 1
            for lo, width in tiles:
                moved = jnp.dot(held[a % 2], rest[:, lo:lo + width], preferred_element_type=jnp.float32)
                value = (now[:, lo:lo + width] + moved) * factor[:, lo:lo + width]
                now[:, lo:lo + width] = value
                held[(a + 1) % 2, :, lo:lo + width] = value.astype(jnp.bfloat16)
                if last:
                    part = value * value
                    total = part[:, :128]
                    for q in range(128, width, 128):
                        total = total + part[:, q:q + 128]
                    squares[...] = total if lo == 0 else squares[...] + total
        summed = lax.dot_general(
            ones, squares[...], (((1,), (1,)), ((), ())),
            precision=lax.Precision.HIGHEST, preferred_element_type=jnp.float32,
        )
        scale = scale_row[...]
        rms = jnp.sqrt(summed * (1.0 / sites) * scale * scale + EPS)
        scale_row[...] = scale / rms
        gained = jnp.log(rms)
        for t in range(STEPS):
            slot = 0 if log_reach[t] == 0 else 1 + log_dist.index(log_reach[t])

            @pl.when(s == t)
            def _(slot=slot, t=t):
                logs[slot] = logs[slot] + gained
                if slot and all(log_reach[u] != log_reach[t] for u in range(t + 1, STEPS)):
                    log_copy(slot - 1).start()

        return carry

    lax.fori_loop(0, STEPS, step, 0)

    sign = 1.0
    for s in range(STEPS):
        slice_at = lax.rem(me + (slices - log_reach[s]) % slices, slices)
        sign = sign * jnp.where(slice_at < 4, -1.0, 1.0)
    pick = jnp.where(lax.broadcasted_iota(jnp.int32, (8, 128), 0) == 0, 1.0, 0.0)
    scale = lax.dot_general(
        scale_row[...], pick, (((0,), (0,)), ((), ())),
        precision=lax.Precision.HIGHEST, preferred_element_type=jnp.float32,
    ) * sign
    for lo in range(0, sites, 128):
        panels_ref[:, lo:lo + 128] = now[:, lo:lo + 128] * scale

    total = logs[0]
    for i in range(len(log_dist)):
        log_copy(i).wait()
        total = total + landed[i]
    growth_ref[...] = total[0:1] * (1.0 / (SPAN * STEPS))


def shards(slices, spins, neighbours, start):
    rows, sites = start.shape
    hops = STEPS * SPAN
    shift = hops % slices
    if shift:
        moved = lax.ppermute(
            start.astype(jnp.bfloat16), "tm", [(i, (i + shift) % slices) for i in range(slices)]
        )
        start = moved.astype(jnp.float32)
    reach = min(hops, slices)
    ways = max(1, len({SPAN * s % slices for s in range(1, STEPS)} - {0}))
    vmem = pl.BlockSpec(memory_space=pltpu.VMEM)
    panels, growth = pl.pallas_call(
        functools.partial(kernel, slices),
        out_shape=(
            jax.ShapeDtypeStruct((rows, sites), jnp.float32),
            jax.ShapeDtypeStruct((1, rows), jnp.float32),
        ),
        in_specs=[vmem, vmem, pl.BlockSpec(memory_space=pl.ANY)],
        out_specs=(vmem, vmem),
        scratch_shapes=[
            pltpu.VMEM((reach, 1, sites), jnp.int32),
            pltpu.VMEM((reach, 1, sites), jnp.float32),
            pltpu.VMEM((sites, sites), jnp.bfloat16),
            pltpu.VMEM((sites, sites), jnp.float8_e4m3fn),
            pltpu.VMEM((sites, sites), jnp.bfloat16),
            pltpu.VMEM((rows, sites), jnp.float32),
            pltpu.VMEM((2, rows, sites), jnp.bfloat16),
            pltpu.VMEM((rows, 128), jnp.float32),
            pltpu.VMEM((1 + ways, 8, rows), jnp.float32),
            pltpu.VMEM((ways, 8, rows), jnp.float32),
            pltpu.VMEM((8, rows), jnp.float32),
            pltpu.SemaphoreType.DMA,
            pltpu.SemaphoreType.DMA((reach,)),
            pltpu.SemaphoreType.DMA((reach,)),
            pltpu.SemaphoreType.DMA((ways,)),
            pltpu.SemaphoreType.DMA((ways,)),
        ],
        compiler_params=pltpu.CompilerParams(
            collective_id=0, has_side_effects=True, vmem_limit_bytes=40 * 1024 * 1024
        ),
        cost_estimate=pl.CostEstimate(
            flops=2 * (hops * rows + sites) * sites * sites,
            bytes_accessed=8 * rows * sites, transcendentals=0,
        ),
    )(spins, neighbours.T, start)
    return panels, growth.reshape(rows)


def solution(mesh):
    return jax.shard_map(
        functools.partial(shards, mesh.shape["tm"]),
        mesh=mesh,
        in_specs=(P("tm", None), P(), P(("tm", "panel"), None)),
        out_specs=(P(("tm", "panel"), None), P(("tm", "panel"))),
        check_vma=False,
    )
```

time: 230 us -> 32.9 us (0.14)
  waiting for transfers between devices: 183 us -> 0 us
  Pallas kernels: 0 us -> 27.6 us
  matrix products: 18.3 us -> 0 us
  between operations: 14.2 us -> 0.65 us
  starting transfers between devices: 5.12 us -> 0 us
    ppermute x7 -> x0, waiting for transfers between devices: 175 us -> none  [from_behind(): lax.ppermute(value, axis, [(i, (i + by) % length) for i in range(length)])]
    pallas_call x0 -> x1, Pallas kernels: none -> 27.6 us  [shards(): pl.pallas_call(functools.partial(kernel, slices), out_shape=(jax.ShapeDty...]
    dot_general x8 -> x0, matrix products: 18.3 us -> none  [the longest x4 6.86 us: shards(): jnp.dot(incoming, full_block, preferred_element_type=jnp.float32) * sign]
    all_gather x2 -> x0, waiting for transfers between devices: 7.62 us -> none  [the longest x1 7.61 us: shards(): hop = lax.all_gather(hop_part, 'panel', axis=0, tiled=True)]
    ppermute x7 -> x0, starting transfers between devices: 5.04 us -> none  [from_behind(): lax.ppermute(value, axis, [(i, (i + by) % length) for i in range(length)])]
    gather x2 -> x0, local copies, waits for them, and re-layouts: 3.5 us -> none  [adjacency(): picked = neighbours[rows]]
    unnamed x9 -> x7, local copies, waits for them, and re-layouts: 0.98 us -> 3.79 us
  transfers between devices with their start and end apart: 9 -> 0, of which waited for: 8 -> 0; matrix products, arithmetic and copies ran while one was open for 0% -> 0% of each run, Pallas kernels for 0% -> 0%
where the time goes in v1:
time: 32.9 us; the launch traced here: 32.7 us
  Pallas kernels  27.6 us (84%)
  local copies, waits for them, and re-layouts  3.79 us (12%)
  between operations  0.65 us (2%)
  other arithmetic  0.6 us (2%)
    pallas_call x1, Pallas kernels, shards(): pl.pallas_call(functools.partial(kernel, slices), out_shape=(jax.ShapeDty...  27.6 us
    unnamed x7, local copies, waits for them, and re-layouts  3.79 us

profile of v1, /device:TPU:0, one launch (start us, length us, event | category | flops | bytes accessed | tf_op | source)
XLA Modules:
  0.0 32.7 jit_solution(7578849861877112379)
XLA Ops:
  0.6 0.0 copy-start
  0.6 1.3 %copy-done = f32[288,1152]{1,0:T(8,128)S(1)} copy-done((f32[288,1152]{1,0:T(8,128)S(1)}, f32[288,1152]{1,0:T(8,128)}, u32[]{:S(2)}) %copy-start) | copy-done | bytes 1327128
  2.0 0.0 copy-start.1
  2.0 0.7 %copy-done.1 = s32[1152,4]{0,1:T(4,128)S(1)} copy-done((s32[1152,4]{0,1:T(4,128)S(1)}, s32[1152,4]{0,1:T(4,128)}, u32[]{:S(2)}) %copy-start.1) | copy-done | bytes 18456
  2.7 0.0 copy-start.2
  2.7 0.7 %copy-done.2 = s32[1,1152]{1,0:T(1,128)S(1)} copy-done((s32[1,1152]{1,0:T(1,128)S(1)}, s32[1,1152]{1,0:T(1,128)}, u32[]{:S(2)}) %copy-start.2) | copy-done | bytes 4632
  3.4 27.6 %shard_map.50 = (f32[288,1152]{1,0:T(8,128)S(1)}, f32[1,288]{1,0:T(1,128)S(1)}) custom-call(s32[1,1152]{1,0:T(1,128)S(1)} %copy-done.2, s32[4,1152]{1,0:T(4,128)S(1)} %bitcast.1, f32[288,1152]{1,0:T(8,128)S(1)} %copy-done), custom_call_target="tpu_custom_call" | custom-call | flops 15288238080 | bytes 2654208 | tf_op jit(solution)/shard_map/pallas_call | solution.py:174
  31.0 0.6 %reduce = f32[288]{0:T(512)} reduce(f32[1,288]{1,0:T(1,128)S(1)} %get-tuple-element.5, f32[]{:T(128)} %constant.1), dimensions={0}, to_apply=%get-tuple-element.5.reduce_sub_computation | reduce | bytes 2308 | tf_op jit(solution)/shard_map/pallas_call | solution.py:174
  31.6 1.1 %copy.6 = f32[288,1152]{1,0:T(8,128)} copy(f32[288,1152]{1,0:T(8,128)S(1)} %get-tuple-element.8) | data formatting | bytes 2654208
Async XLA Ops:
  0.6 1.3 %copy-start = (f32[288,1152]{1,0:T(8,128)S(1)}, f32[288,1152]{1,0:T(8,128)}, u32[]{:S(2)}) copy-start(f32[288,1152]{1,0:T(8,128)} %start_ref.1) | copy-start | bytes 3981316
  2.0 0.7 %copy-start.1 = (s32[1152,4]{0,1:T(4,128)S(1)}, s32[1152,4]{0,1:T(4,128)}, u32[]{:S(2)}) copy-start(s32[1152,4]{0,1:T(4,128)} %param.4) | copy-start | bytes 55300
  2.7 0.7 %copy-start.2 = (s32[1,1152]{1,0:T(1,128)S(1)}, s32[1,1152]{1,0:T(1,128)}, u32[]{:S(2)}) copy-start(s32[1,1152]{1,0:T(1,128)} %spins_ref.1) | copy-start | bytes 13828

commit v2 on v1

--- a/solution.py
+++ b/solution.py
@@ -22,8 +22,8 @@
 
 def kernel(
     slices, spins_ref, table_ref, start_ref, panels_ref, growth_ref,
-    spins_all, factors, bonds, bonds8, rest, now, held, squares, logs, landed, scale_row,
-    start_sem, spin_send, spin_recv, log_send, log_recv,
+    spins_all, table, factors, bonds, bonds8, rest, now, held, squares, logs, landed, scale_row,
+    fetch_sem, store_sem, spin_send, spin_recv, log_send, log_recv,
 ):
     rows, sites = now.shape
     hops = STEPS * SPAN
@@ -37,7 +37,11 @@
     log_reach = [SPAN * (STEPS - 1 - s) % slices for s in range(STEPS)]
     log_dist = sorted({d for d in log_reach if d != 0})
 
-    fetch = pltpu.make_async_copy(start_ref, now, start_sem)
+    fetch_table = pltpu.make_async_copy(table_ref, table, fetch_sem.at[0])
+    fetch_spins = pltpu.make_async_copy(spins_ref, spins_all.at[0], fetch_sem.at[1])
+    fetch = pltpu.make_async_copy(start_ref, now, fetch_sem.at[2])
+    fetch_table.start()
+    fetch_spins.start()
     fetch.start()
 
     targets = set(range(1, spin_reach)) | {slices - d for d in log_dist}
@@ -45,16 +49,16 @@
     barrier = pltpu.get_barrier_semaphore()
     for offset in greeted:
         pl.semaphore_signal(barrier, inc=1, device_id=at(offset), device_id_type=MESH)
-    spins_all[0] = spins_ref[...]
+    fetch_table.wait()
 
     chunk = rows // 3
 
     def build(c, carry):
         first = pl.multiple_of(c * chunk, chunk)
         label = lax.broadcasted_iota(jnp.int32, (chunk, sites), 0) + first
-        hit = table_ref[0:1, :] == label
+        hit = table[0:1, :] == label
         for k in range(1, 4):
-            hit = hit | (table_ref[k:k + 1, :] == label)
+            hit = hit | (table[k:k + 1, :] == label)
         value = jnp.where(hit, DTAU, 0.0)
         bonds[pl.ds(first, chunk), :] = value.astype(jnp.bfloat16)
         bonds8[pl.ds(first, chunk), :] = value.astype(bonds8.dtype)
@@ -62,6 +66,7 @@
 
     lax.fori_loop(0, sites // chunk, build, 0)
 
+    fetch_spins.wait()
     pl.semaphore_wait(barrier, len(greeted))
     sends = []
     for d in range(1, spin_reach):
@@ -94,8 +99,6 @@
 
     scale_row[...] = jnp.ones_like(scale_row)
     logs[...] = jnp.zeros_like(logs)
-    ones = jnp.ones((8, 128), jnp.float32)
-
     def log_copy(i):
         return pltpu.make_async_remote_copy(
             src_ref=logs.at[1 + i], dst_ref=landed.at[i],
@@ -103,10 +106,9 @@
             device_id=at(slices - log_dist[i]), device_id_type=MESH,
         )
 
-    def step(s, carry):
+    def advance(s):
         for a in range(SPAN):
-            behind = lax.rem(hops - 1 - SPAN * s - a, slices)
-            factor = factors.at[behind]
+            factor = factors.at[lax.rem(hops - 1 - SPAN * s - a, slices)]
             last = a == SPAN - 1
             for lo, width in tiles:
                 moved = jnp.dot(held[a % 2], rest[:, lo:lo + width], preferred_element_type=jnp.float32)
@@ -119,26 +121,45 @@
                     for q in range(128, width, 128):
                         total = total + part[:, q:q + 128]
                     squares[...] = total if lo == 0 else squares[...] + total
-        summed = lax.dot_general(
-            ones, squares[...], (((1,), (1,)), ((), ())),
-            precision=lax.Precision.HIGHEST, preferred_element_type=jnp.float32,
-        )
+
+    def row_sums(values):
+        high = values.astype(jnp.bfloat16)
+        low = (values - high.astype(jnp.float32)).astype(jnp.bfloat16)
+        ones = jnp.ones((16, 128), jnp.bfloat16)
+        over = (((1,), (1,)), ((), ()))
+        return (
+            lax.dot_general(ones, high, over, preferred_element_type=jnp.float32)
+            + lax.dot_general(ones, low, over, preferred_element_type=jnp.float32)
+        )[:8]
+
+    def account(s):
         scale = scale_row[...]
-        rms = jnp.sqrt(summed * (1.0 / sites) * scale * scale + EPS)
+        rms = jnp.sqrt(row_sums(squares[...]) * (1.0 / sites) * scale * scale + EPS)
         scale_row[...] = scale / rms
         gained = jnp.log(rms)
-        for t in range(STEPS):
-            slot = 0 if log_reach[t] == 0 else 1 + log_dist.index(log_reach[t])
-
-            @pl.when(s == t)
-            def _(slot=slot, t=t):
-                logs[slot] = logs[slot] + gained
-                if slot and all(log_reach[u] != log_reach[t] for u in range(t + 1, STEPS)):
-                    log_copy(slot - 1).start()
-
+        for slot in range(1 + len(log_dist)):
+            distance = 0 if slot == 0 else log_dist[slot - 1]
+            steps_of = [t for t in range(STEPS) if log_reach[t] == distance]
+            if isinstance(s, int):
+                if s in steps_of:
+                    logs[slot] = logs[slot] + gained
+            else:
+                member = functools.reduce(jnp.logical_or, [s == t for t in steps_of])
+                logs[slot] = logs[slot] + jnp.where(member, gained, 0.0)
+
+    advance(0)
+
+    def step(s, carry):
+        account(s - 1)
+        advance(s)
         return carry
 
-    lax.fori_loop(0, STEPS, step, 0)
+    lax.fori_loop(1, STEPS - 1, step, 0)
+    account(STEPS - 2)
+    for i in range(len(log_dist)):
+        log_copy(i).start()
+    advance(STEPS - 1)
+    account(STEPS - 1)
 
     sign = 1.0
     for s in range(STEPS):
@@ -149,14 +170,21 @@
         scale_row[...], pick, (((0,), (0,)), ((), ())),
         precision=lax.Precision.HIGHEST, preferred_element_type=jnp.float32,
     ) * sign
-    for lo in range(0, sites, 128):
-        panels_ref[:, lo:lo + 128] = now[:, lo:lo + 128] * scale
+    parts = []
+    for c in range(3):
+        part = pl.ds(c * chunk, chunk)
+        for lo in range(0, sites, 128):
+            now[part, lo:lo + 128] = now[part, lo:lo + 128] * scale[c * chunk:(c + 1) * chunk]
+        parts.append(pltpu.make_async_copy(now.at[part], panels_ref.at[part], store_sem.at[c]))
+        parts[-1].start()
 
     total = logs[0]
     for i in range(len(log_dist)):
         log_copy(i).wait()
         total = total + landed[i]
     growth_ref[...] = total[0:1] * (1.0 / (SPAN * STEPS))
+    for part in parts:
+        part.wait()
 
 
 def shards(slices, spins, neighbours, start):
@@ -177,10 +205,11 @@
             jax.ShapeDtypeStruct((rows, sites), jnp.float32),
             jax.ShapeDtypeStruct((1, rows), jnp.float32),
         ),
-        in_specs=[vmem, vmem, pl.BlockSpec(memory_space=pl.ANY)],
-        out_specs=(vmem, vmem),
+        in_specs=[pl.BlockSpec(memory_space=pltpu.HBM)] * 3,
+        out_specs=(pl.BlockSpec(memory_space=pltpu.HBM), vmem),
         scratch_shapes=[
             pltpu.VMEM((reach, 1, sites), jnp.int32),
+            pltpu.VMEM((4, sites), jnp.int32),
             pltpu.VMEM((reach, 1, sites), jnp.float32),
             pltpu.VMEM((sites, sites), jnp.bfloat16),
             pltpu.VMEM((sites, sites), jnp.float8_e4m3fn),
@@ -191,14 +220,15 @@
             pltpu.VMEM((1 + ways, 8, rows), jnp.float32),
             pltpu.VMEM((ways, 8, rows), jnp.float32),
             pltpu.VMEM((8, rows), jnp.float32),
-            pltpu.SemaphoreType.DMA,
+            pltpu.SemaphoreType.DMA((3,)),
+            pltpu.SemaphoreType.DMA((3,)),
             pltpu.SemaphoreType.DMA((reach,)),
             pltpu.SemaphoreType.DMA((reach,)),
             pltpu.SemaphoreType.DMA((ways,)),
             pltpu.SemaphoreType.DMA((ways,)),
         ],
         compiler_params=pltpu.CompilerParams(
-            collective_id=0, has_side_effects=True, vmem_limit_bytes=40 * 1024 * 1024
+            collective_id=0, has_side_effects=True, vmem_limit_bytes=64 * 1024 * 1024
         ),
         cost_estimate=pl.CostEstimate(
             flops=2 * (hops * rows + sites) * sites * sites,

time: 32.9 us -> 33.7 us (1.024)
  Pallas kernels: 27.6 us -> 29.2 us
  local copies, waits for them, and re-layouts: 3.79 us -> 2.47 us
  other arithmetic: 0.6 us -> 1.25 us
    pallas_call x1, Pallas kernels: 27.6 us -> 29.2 us  [shards(): pl.pallas_call(functools.partial(kernel, slices), out_shape=(jax.ShapeDty...]
    unnamed x7 -> x1, local copies, waits for them, and re-layouts: 3.79 us -> 2.47 us
    pallas_call x1, other arithmetic: 0.6 us -> 1.25 us  [shards(): pl.pallas_call(functools.partial(kernel, slices), out_shape=(jax.ShapeDty...]
where the time goes in v2:
time: 33.7 us; the launch traced here: 33.5 us
  Pallas kernels  29.2 us (87%)
  local copies, waits for them, and re-layouts  2.47 us (7%)
  other arithmetic  1.25 us (4%)
  between operations  0.64 us (2%)
    pallas_call x1, Pallas kernels, shards(): pl.pallas_call(functools.partial(kernel, slices), out_shape=(jax.ShapeDty...  29.2 us
    unnamed x1, local copies, waits for them, and re-layouts  2.47 us
    pallas_call x1, other arithmetic, shards(): pl.pallas_call(functools.partial(kernel, slices), out_shape=(jax.ShapeDty...  1.25 us

profile of v2, /device:TPU:0, one launch (start us, length us, event | category | flops | bytes accessed | tf_op | source)
XLA Modules:
  0.0 33.5 jit_solution(15313530370405131385)
XLA Ops:
  0.6 29.2 %shard_map.50 = (f32[288,1152]{1,0:T(8,128)}, f32[1,288]{1,0:T(1,128)}) custom-call(s32[1,1152]{1,0:T(1,128)} %spins_ref.1, s32[4,1152]{1,0:T(4,128)} %bitcast.1, f32[288,1152]{1,0:T(8,128)} %start_ref.1), custom_call_target="tpu_custom_call" | custom-call | flops 15288238080 | bytes 2654208 | tf_op jit(solution)/shard_map/pallas_call | solution.py:202
  29.8 1.3 %reduce = f32[288]{0:T(512)} reduce(f32[1,288]{1,0:T(1,128)} %get-tuple-element.5, f32[]{:T(128)} %constant.1), dimensions={0}, to_apply=%get-tuple-element.5.reduce_sub_computation | reduce | bytes 2308 | tf_op jit(solution)/shard_map/pallas_call | solution.py:202
  31.1 2.5 %copy.6 = f32[288,1152]{1,0:T(8,128)} copy(f32[288,1152]{1,0:T(8,128)} %get-tuple-element.8) | data formatting | bytes 2654208

commit v3 on v2

--- a/solution.py
+++ b/solution.py
@@ -12,7 +12,7 @@
 DTAU = 0.0625
 LAMBDA = 0.5
 EPS = 1e-06
-TILE = 256
+TILE = 1152
 MESH = pl.DeviceIdType.MESH
 
 
@@ -21,9 +21,9 @@
 
 
 def kernel(
-    slices, spins_ref, table_ref, start_ref, panels_ref, growth_ref,
-    spins_all, table, factors, bonds, bonds8, rest, now, held, squares, logs, landed, scale_row,
-    fetch_sem, store_sem, spin_send, spin_recv, log_send, log_recv,
+    slices, table, start_ref, panels_ref, growth_ref,
+    spins_all, factors, bonds, bonds8, rest, now, held, squares, logs, landed, scale_row,
+    fetch_sem, spin_send, spin_recv, log_send, log_recv,
 ):
     rows, sites = now.shape
     hops = STEPS * SPAN
@@ -37,11 +37,7 @@
     log_reach = [SPAN * (STEPS - 1 - s) % slices for s in range(STEPS)]
     log_dist = sorted({d for d in log_reach if d != 0})
 
-    fetch_table = pltpu.make_async_copy(table_ref, table, fetch_sem.at[0])
-    fetch_spins = pltpu.make_async_copy(spins_ref, spins_all.at[0], fetch_sem.at[1])
-    fetch = pltpu.make_async_copy(start_ref, now, fetch_sem.at[2])
-    fetch_table.start()
-    fetch_spins.start()
+    fetch = pltpu.make_async_copy(start_ref, now, fetch_sem)
     fetch.start()
 
     targets = set(range(1, spin_reach)) | {slices - d for d in log_dist}
@@ -49,7 +45,7 @@
     barrier = pltpu.get_barrier_semaphore()
     for offset in greeted:
         pl.semaphore_signal(barrier, inc=1, device_id=at(offset), device_id_type=MESH)
-    fetch_table.wait()
+    spins_all[0] = table[4:5, :]
 
     chunk = rows // 3
 
@@ -66,7 +62,6 @@
 
     lax.fori_loop(0, sites // chunk, build, 0)
 
-    fetch_spins.wait()
     pl.semaphore_wait(barrier, len(greeted))
     sends = []
     for d in range(1, spin_reach):
@@ -170,21 +165,14 @@
         scale_row[...], pick, (((0,), (0,)), ((), ())),
         precision=lax.Precision.HIGHEST, preferred_element_type=jnp.float32,
     ) * sign
-    parts = []
-    for c in range(3):
-        part = pl.ds(c * chunk, chunk)
-        for lo in range(0, sites, 128):
-            now[part, lo:lo + 128] = now[part, lo:lo + 128] * scale[c * chunk:(c + 1) * chunk]
-        parts.append(pltpu.make_async_copy(now.at[part], panels_ref.at[part], store_sem.at[c]))
-        parts[-1].start()
+    for lo in range(0, sites, 128):
+        panels_ref[:, lo:lo + 128] = now[:, lo:lo + 128] * scale
 
     total = logs[0]
     for i in range(len(log_dist)):
         log_copy(i).wait()
         total = total + landed[i]
     growth_ref[...] = total[0:1] * (1.0 / (SPAN * STEPS))
-    for part in parts:
-        part.wait()
 
 
 def shards(slices, spins, neighbours, start):
@@ -205,11 +193,10 @@
             jax.ShapeDtypeStruct((rows, sites), jnp.float32),
             jax.ShapeDtypeStruct((1, rows), jnp.float32),
         ),
-        in_specs=[pl.BlockSpec(memory_space=pltpu.HBM)] * 3,
-        out_specs=(pl.BlockSpec(memory_space=pltpu.HBM), vmem),
+        in_specs=[vmem, pl.BlockSpec(memory_space=pl.ANY)],
+        out_specs=(vmem, vmem),
         scratch_shapes=[
             pltpu.VMEM((reach, 1, sites), jnp.int32),
-            pltpu.VMEM((4, sites), jnp.int32),
             pltpu.VMEM((reach, 1, sites), jnp.float32),
             pltpu.VMEM((sites, sites), jnp.bfloat16),
             pltpu.VMEM((sites, sites), jnp.float8_e4m3fn),
@@ -220,21 +207,20 @@
             pltpu.VMEM((1 + ways, 8, rows), jnp.float32),
             pltpu.VMEM((ways, 8, rows), jnp.float32),
             pltpu.VMEM((8, rows), jnp.float32),
-            pltpu.SemaphoreType.DMA((3,)),
-            pltpu.SemaphoreType.DMA((3,)),
+            pltpu.SemaphoreType.DMA,
             pltpu.SemaphoreType.DMA((reach,)),
             pltpu.SemaphoreType.DMA((reach,)),
             pltpu.SemaphoreType.DMA((ways,)),
             pltpu.SemaphoreType.DMA((ways,)),
         ],
         compiler_params=pltpu.CompilerParams(
-            collective_id=0, has_side_effects=True, vmem_limit_bytes=64 * 1024 * 1024
+            collective_id=0, has_side_effects=True, vmem_limit_bytes=52 * 1024 * 1024
         ),
         cost_estimate=pl.CostEstimate(
             flops=2 * (hops * rows + sites) * sites * sites,
             bytes_accessed=8 * rows * sites, transcendentals=0,
         ),
-    )(spins, neighbours.T, start)
+    )(jnp.concatenate([neighbours.T, spins], axis=0), start)
     return panels, growth.reshape(rows)
 
 

time: 33.7 us -> 30.2 us (0.90)
  Pallas kernels: 29.2 us -> 26.9 us
  local copies, waits for them, and re-layouts: 2.47 us -> 1.06 us
    pallas_call x1, Pallas kernels: 29.2 us -> 26.9 us  [shards(): pl.pallas_call(functools.partial(kernel, slices), out_shape=(jax.ShapeDty...]
    unnamed x1, local copies, waits for them, and re-layouts: 2.47 us -> 1.06 us
    concatenate x0 -> x1, other arithmetic: none -> 0.75 us  [shards(): jnp.concatenate([neighbours.T, spins], axis=0)]
    pallas_call x1, other arithmetic: 1.25 us -> 0.6 us  [shards(): pl.pallas_call(functools.partial(kernel, slices), out_shape=(jax.ShapeDty...]
where the time goes in v3:
time: 30.2 us; the launch traced here: 30 us
  Pallas kernels  26.9 us (89%)
  other arithmetic  1.35 us (4%)
  local copies, waits for them, and re-layouts  1.06 us (4%)
  between operations  0.64 us (2%)
    pallas_call x1, Pallas kernels, shards(): pl.pallas_call(functools.partial(kernel, slices), out_shape=(jax.ShapeDty...  26.9 us
    unnamed x1, local copies, waits for them, and re-layouts  1.06 us
    concatenate x1, other arithmetic, shards(): jnp.concatenate([neighbours.T, spins], axis=0)  0.75 us

profile of v3, /device:TPU:0, one launch (start us, length us, event | category | flops | bytes accessed | tf_op | source)
XLA Modules:
  0.0 30.0 jit_solution(346552105889404511)
XLA Ops:
  0.6 0.8 %pad_add_fusion.table = s32[5,1152]{1,0:T(8,128)S(1)} fusion(s32[1,1152]{1,0:T(1,128)} %param.3, s32[4,1152]{1,0:T(4,128)} %bitcast.1), kind=kLoop, calls=%fused_computation | loop fusion | flops 5760 | bytes 46080 | tf_op jit(solution)/shard_map/concatenate | solution.py:223
  1.4 26.9 %shard_map.50 = (f32[288,1152]{1,0:T(8,128)S(1)}, f32[1,288]{1,0:T(1,128)S(1)}) custom-call(s32[5,1152]{1,0:T(8,128)S(1)} %pad_add_fusion.table, f32[288,1152]{1,0:T(8,128)} %start_ref.1), custom_call_target="tpu_custom_call" | custom-call | flops 15288238080 | bytes 2654208 | tf_op jit(solution)/shard_map/pallas_call | solution.py:190
  28.3 0.6 %reduce = f32[288]{0:T(512)} reduce(f32[1,288]{1,0:T(1,128)S(1)} %get-tuple-element.5, f32[]{:T(128)} %constant.1), dimensions={0}, to_apply=%get-tuple-element.5.reduce_sub_computation | reduce | bytes 2308 | tf_op jit(solution)/shard_map/pallas_call | solution.py:190
  28.9 1.1 %copy.6 = f32[288,1152]{1,0:T(8,128)} copy(f32[288,1152]{1,0:T(8,128)S(1)} %get-tuple-element.8) | data formatting | bytes 2654208

commit v4 on v1

v4 whole, which is shorter than its diff:
```python
import functools

import jax
import jax.numpy as jnp
from jax import lax
from jax.experimental import pallas as pl
from jax.experimental.pallas import tpu as pltpu
from jax.sharding import PartitionSpec as P

STEPS = 4
SPAN = 4
DTAU = 0.0625
LAMBDA = 0.5
EPS = 1e-06
TILE = 1152
COARSE = 8
LEVEL = 0.0625
CARRY = 1.1276
MESH = pl.DeviceIdType.MESH


def column_tiles(sites):
    return [(at, min(TILE, sites - at)) for at in range(0, sites, TILE)]


def kernel(
    slices, table, start_ref, panels_ref, growth_ref,
    spins_all, factors, bonds, bonds8, rest, rest8, now, held, held8, owed, squares, logs, landed, scale_row,
    fetch_sem, spin_send, spin_recv, log_send, log_recv,
):
    rows, sites = now.shape
    hops = STEPS * SPAN
    tiles = column_tiles(sites)
    me = lax.axis_index("tm")

    def at(offset):
        return {"tm": lax.rem(me + (offset % slices), slices)}

    spin_reach = min(hops, slices)
    log_reach = [SPAN * (STEPS - 1 - s) % slices for s in range(STEPS)]
    log_dist = sorted({d for d in log_reach if d != 0})

    fetch = pltpu.make_async_copy(start_ref, now, fetch_sem)
    fetch.start()

    targets = set(range(1, spin_reach)) | {slices - d for d in log_dist}
    greeted = sorted(targets | {slices - d for d in targets})
    barrier = pltpu.get_barrier_semaphore()
    for offset in greeted:
        pl.semaphore_signal(barrier, inc=1, device_id=at(offset), device_id_type=MESH)
    spins_all[0] = table[4:5, :]

    chunk = rows // 3

    def build(c, carry):
        first = pl.multiple_of(c * chunk, chunk)
        label = lax.broadcasted_iota(jnp.int32, (chunk, sites), 0) + first
        hit = table[0:1, :] == label
        for k in range(1, 4):
            hit = hit | (table[k:k + 1, :] == label)
        value = jnp.where(hit, DTAU, 0.0)
        bonds[pl.ds(first, chunk), :] = value.astype(jnp.bfloat16)
        bonds8[pl.ds(first, chunk), :] = value.astype(bonds8.dtype)
        return carry

    lax.fori_loop(0, sites // chunk, build, 0)

    pl.semaphore_wait(barrier, len(greeted))
    sends = []
    for d in range(1, spin_reach):
        copy = pltpu.make_async_remote_copy(
            src_ref=spins_all.at[0], dst_ref=spins_all.at[d],
            send_sem=spin_send.at[d], recv_sem=spin_recv.at[d],
            device_id=at(d), device_id_type=MESH,
        )
        copy.start()
        sends.append(copy)

    def row_sums(values):
        high = values.astype(jnp.bfloat16)
        low = (values - high.astype(jnp.float32)).astype(jnp.bfloat16)
        ones = jnp.ones((16, 128), jnp.bfloat16)
        over = (((1,), (1,)), ((), ()))
        return (
            lax.dot_general(ones, high, over, preferred_element_type=jnp.float32)
            + lax.dot_general(ones, low, over, preferred_element_type=jnp.float32)
        )[:8]

    def to_column(line):
        pick = jnp.where(lax.broadcasted_iota(jnp.int32, (8, 128), 0) == 0, 1.0, 0.0)
        return lax.dot_general(
            line, pick, (((0,), (0,)), ((), ())),
            precision=lax.Precision.HIGHEST, preferred_element_type=jnp.float32,
        )

    def square(c, carry):
        first = pl.multiple_of(c * rows, rows)
        block = pl.ds(first, rows)
        for lo, width in tiles:
            twice = jnp.dot(bonds8[block, :], bonds8[:, lo:lo + width], preferred_element_type=jnp.float32)
            one = bonds[block, lo:lo + width].astype(jnp.float32)
            both = one + 0.5 * twice
            rest[block, lo:lo + width] = both.astype(jnp.bfloat16)
            rest8[block, lo:lo + width] = (both * 512.0).astype(rest8.dtype)
        return carry

    lax.fori_loop(0, sites // rows, square, 0)

    fetch.wait()
    for lo in range(0, sites, 128):
        value = now[:, lo:lo + 128].astype(jnp.bfloat16).astype(jnp.float32)
        now[:, lo:lo + 128] = value
        squares[...] = value * value if lo == 0 else squares[...] + value * value
    level = jnp.sqrt(row_sums(squares[...]) * (1.0 / sites) + 1e-30) * (1.0 / LEVEL)
    scale_row[...] = level
    scale = to_column(1.0 / level)
    for lo in range(0, sites, 128):
        value = now[:, lo:lo + 128] * scale
        now[:, lo:lo + 128] = value
        eighth = value.astype(held8.dtype)
        held8[0, :, lo:lo + 128] = eighth
        owed[:, lo:lo + 128] = (value - eighth.astype(jnp.float32)) * CARRY

    for copy in sends:
        copy.wait()
    factors[...] = jnp.exp(LAMBDA * spins_all[...].astype(jnp.float32))

    logs[...] = jnp.zeros_like(logs)
    def log_copy(i):
        return pltpu.make_async_remote_copy(
            src_ref=logs.at[1 + i], dst_ref=landed.at[i],
            send_sem=log_send.at[i], recv_sem=log_recv.at[i],
            device_id=at(slices - log_dist[i]), device_id_type=MESH,
        )

    def advance(s, coarse):
        for a in range(SPAN):
            factor = factors.at[lax.rem(hops - 1 - SPAN * s - a, slices)]
            last = a == SPAN - 1
            for lo, width in tiles:
                span = slice(lo, lo + width)
                if coarse:
                    moved = jnp.dot(held8[a % 2], rest8[:, span], preferred_element_type=jnp.float32) * (1.0 / 512.0)
                else:
                    moved = jnp.dot(held[a % 2], rest[:, span], preferred_element_type=jnp.float32)
                value = (now[:, span] + moved) * factor[:, span]
                now[:, span] = value
                if coarse:
                    wanted = value + owed[:, span]
                    if last and (s + 1) * SPAN == COARSE:
                        held[0, :, span] = wanted.astype(jnp.bfloat16)
                    else:
                        eighth = wanted.astype(held8.dtype)
                        held8[(a + 1) % 2, :, span] = eighth
                        owed[:, span] = (wanted - eighth.astype(jnp.float32)) * CARRY
                else:
                    held[(a + 1) % 2, :, span] = value.astype(jnp.bfloat16)
                if last:
                    part = value * value
                    total = part[:, :128]
                    for q in range(128, width, 128):
                        total = total + part[:, q:q + 128]
                    squares[...] = total if lo == 0 else squares[...] + total

    def account(s):
        scale = scale_row[...]
        rms = jnp.sqrt(row_sums(squares[...]) * (1.0 / sites) * scale * scale + EPS)
        scale_row[...] = scale / rms
        gained = jnp.log(rms)
        for slot in range(1 + len(log_dist)):
            distance = 0 if slot == 0 else log_dist[slot - 1]
            steps_of = [t for t in range(STEPS) if log_reach[t] == distance]
            if s in steps_of:
                logs[slot] = logs[slot] + gained

    for s in range(STEPS):
        advance(s, s * SPAN < COARSE)
        account(s)
        if s == STEPS - 2:
            for i in range(len(log_dist)):
                log_copy(i).start()

    sign = 1.0
    for s in range(STEPS):
        slice_at = lax.rem(me + (slices - log_reach[s]) % slices, slices)
        sign = sign * jnp.where(slice_at < 4, -1.0, 1.0)
    scale = to_column(scale_row[...]) * sign
    for lo in range(0, sites, 128):
        panels_ref[:, lo:lo + 128] = now[:, lo:lo + 128] * scale

    total = logs[0]
    for i in range(len(log_dist)):
        log_copy(i).wait()
        total = total + landed[i]
    growth_ref[...] = total[0:1] * (1.0 / (SPAN * STEPS))


def shards(slices, spins, neighbours, start):
    rows, sites = start.shape
    hops = STEPS * SPAN
    shift = hops % slices
    if shift:
        moved = lax.ppermute(
            start.astype(jnp.bfloat16), "tm", [(i, (i + shift) % slices) for i in range(slices)]
        )
        start = moved.astype(jnp.float32)
    reach = min(hops, slices)
    ways = max(1, len({SPAN * s % slices for s in range(1, STEPS)} - {0}))
    vmem = pl.BlockSpec(memory_space=pltpu.VMEM)
    panels, growth = pl.pallas_call(
        functools.partial(kernel, slices),
        out_shape=(
            jax.ShapeDtypeStruct((rows, sites), jnp.float32),
            jax.ShapeDtypeStruct((1, rows), jnp.float32),
        ),
        in_specs=[vmem, pl.BlockSpec(memory_space=pl.ANY)],
        out_specs=(vmem, vmem),
        scratch_shapes=[
            pltpu.VMEM((reach, 1, sites), jnp.int32),
            pltpu.VMEM((reach, 1, sites), jnp.float32),
            pltpu.VMEM((sites, sites), jnp.bfloat16),
            pltpu.VMEM((sites, sites), jnp.float8_e4m3fn),
            pltpu.VMEM((sites, sites), jnp.bfloat16),
            pltpu.VMEM((sites, sites), jnp.float8_e4m3fn),
            pltpu.VMEM((rows, sites), jnp.float32),
            pltpu.VMEM((2, rows, sites), jnp.bfloat16),
            pltpu.VMEM((2, rows, sites), jnp.float8_e4m3fn),
            pltpu.VMEM((rows, sites), jnp.float32),
            pltpu.VMEM((rows, 128), jnp.float32),
            pltpu.VMEM((1 + ways, 8, rows), jnp.float32),
            pltpu.VMEM((ways, 8, rows), jnp.float32),
            pltpu.VMEM((8, rows), jnp.float32),
            pltpu.SemaphoreType.DMA,
            pltpu.SemaphoreType.DMA((reach,)),
            pltpu.SemaphoreType.DMA((reach,)),
            pltpu.SemaphoreType.DMA((ways,)),
            pltpu.SemaphoreType.DMA((ways,)),
        ],
        compiler_params=pltpu.CompilerParams(
            collective_id=0, has_side_effects=True, vmem_limit_bytes=52 * 1024 * 1024
        ),
        cost_estimate=pl.CostEstimate(
            flops=2 * (hops * rows + sites) * sites * sites,
            bytes_accessed=8 * rows * sites, transcendentals=0,
        ),
    )(jnp.concatenate([neighbours.T, spins], axis=0), start)
    return panels, growth.reshape(rows)


def solution(mesh):
    return jax.shard_map(
        functools.partial(shards, mesh.shape["tm"]),
        mesh=mesh,
        in_specs=(P("tm", None), P(), P(("tm", "panel"), None)),
        out_specs=(P(("tm", "panel"), None), P(("tm", "panel"))),
        check_vma=False,
    )
```

time: 32.9 us -> 27.1 us (0.82)
  Pallas kernels: 27.6 us -> 23.9 us
  local copies, waits for them, and re-layouts: 3.79 us -> 1.06 us
  other arithmetic: 0.6 us -> 1.35 us
    pallas_call x1, Pallas kernels: 27.6 us -> 23.9 us  [shards(): pl.pallas_call(functools.partial(kernel, slices), out_shape=(jax.ShapeDty...]
    unnamed x7 -> x1, local copies, waits for them, and re-layouts: 3.79 us -> 1.06 us
    concatenate x0 -> x1, other arithmetic: none -> 0.75 us  [shards(): jnp.concatenate([neighbours.T, spins], axis=0)]
where the time goes in v4:
time: 27.1 us; the launch traced here: 26.9 us
  Pallas kernels  23.9 us (88%)
  other arithmetic  1.35 us (5%)
  local copies, waits for them, and re-layouts  1.06 us (4%)
  between operations  0.64 us (2%)
    pallas_call x1, Pallas kernels, shards(): pl.pallas_call(functools.partial(kernel, slices), out_shape=(jax.ShapeDty...  23.9 us
    unnamed x1, local copies, waits for them, and re-layouts  1.06 us
    concatenate x1, other arithmetic, shards(): jnp.concatenate([neighbours.T, spins], axis=0)  0.75 us
    pallas_call x1, other arithmetic, shards(): pl.pallas_call(functools.partial(kernel, slices), out_shape=(jax.ShapeDty...  0.6 us

profile of v4, /device:TPU:0, one launch (start us, length us, event | category | flops | bytes accessed | tf_op | source)
XLA Modules:
  0.0 26.9 jit_solution(16582135032485858678)
XLA Ops:
  0.6 0.8 %pad_add_fusion.table = s32[5,1152]{1,0:T(8,128)S(1)} fusion(s32[1,1152]{1,0:T(1,128)} %param.3, s32[4,1152]{1,0:T(4,128)} %bitcast.1), kind=kLoop, calls=%fused_computation | loop fusion | flops 5760 | bytes 46080 | tf_op jit(solution)/shard_map/concatenate | solution.py:246
  1.4 23.9 %shard_map.50 = (f32[288,1152]{1,0:T(8,128)S(1)}, f32[1,288]{1,0:T(1,128)S(1)}) custom-call(s32[5,1152]{1,0:T(8,128)S(1)} %pad_add_fusion.table, f32[288,1152]{1,0:T(8,128)} %start_ref.1), custom_call_target="tpu_custom_call" | custom-call | flops 15288238080 | bytes 2654208 | tf_op jit(solution)/shard_map/pallas_call | solution.py:210
  25.3 0.6 %reduce = f32[288]{0:T(512)} reduce(f32[1,288]{1,0:T(1,128)S(1)} %get-tuple-element.5, f32[]{:T(128)} %constant.1), dimensions={0}, to_apply=%get-tuple-element.5.reduce_sub_computation | reduce | bytes 2308 | tf_op jit(solution)/shard_map/pallas_call | solution.py:210
  25.9 1.1 %copy.6 = f32[288,1152]{1,0:T(8,128)} copy(f32[288,1152]{1,0:T(8,128)S(1)} %get-tuple-element.8) | data formatting | bytes 2654208

commit v5 on v4

--- a/solution.py
+++ b/solution.py
@@ -13,8 +13,9 @@
 LAMBDA = 0.5
 EPS = 1e-06
 TILE = 1152
-COARSE = 8
+COARSE = 15
 LEVEL = 0.0625
+LEVEL_LATER = 0.015625
 CARRY = 1.1276
 MESH = pl.DeviceIdType.MESH
 
@@ -25,7 +26,7 @@
 
 def kernel(
     slices, table, start_ref, panels_ref, growth_ref,
-    spins_all, factors, bonds, bonds8, rest, rest8, now, held, held8, owed, squares, logs, landed, scale_row,
+    spins_all, factors, bonds, bonds8, rest, rest8, now, held, held8, owed, squares, logs, landed, scale_row, level_row,
     fetch_sem, spin_send, spin_recv, log_send, log_recv,
 ):
     rows, sites = now.shape
@@ -133,28 +134,36 @@
             device_id=at(slices - log_dist[i]), device_id_type=MESH,
         )
 
-    def advance(s, coarse):
+    def advance(s):
         for a in range(SPAN):
-            factor = factors.at[lax.rem(hops - 1 - SPAN * s - a, slices)]
+            hop = s * SPAN + a
+            coarse, coarse_next = hop < COARSE, hop + 1 < COARSE
+            factor = factors.at[lax.rem(hops - 1 - hop, slices)]
             last = a == SPAN - 1
+            rescale = last and s == 1
+            if rescale:
+                column = to_column(level_row[...])
+                scale_row[...] = scale_row[...] / level_row[...]
             for lo, width in tiles:
                 span = slice(lo, lo + width)
                 if coarse:
-                    moved = jnp.dot(held8[a % 2], rest8[:, span], preferred_element_type=jnp.float32) * (1.0 / 512.0)
+                    moved = jnp.dot(held8[hop % 2], rest8[:, span], preferred_element_type=jnp.float32) * (1.0 / 512.0)
                 else:
-                    moved = jnp.dot(held[a % 2], rest[:, span], preferred_element_type=jnp.float32)
+                    moved = jnp.dot(held[hop % 2], rest[:, span], preferred_element_type=jnp.float32)
                 value = (now[:, span] + moved) * factor[:, span]
+                debt = owed[:, span] if coarse else None
+                if rescale:
+                    wide = jnp.concatenate([column] * (width // 128), axis=1)
+                    value = value * wide
+                    debt = debt * wide
                 now[:, span] = value
-                if coarse:
-                    wanted = value + owed[:, span]
-                    if last and (s + 1) * SPAN == COARSE:
-                        held[0, :, span] = wanted.astype(jnp.bfloat16)
-                    else:
-                        eighth = wanted.astype(held8.dtype)
-                        held8[(a + 1) % 2, :, span] = eighth
-                        owed[:, span] = (wanted - eighth.astype(jnp.float32)) * CARRY
-                else:
-                    held[(a + 1) % 2, :, span] = value.astype(jnp.bfloat16)
+                wanted = value + debt if coarse else value
+                if coarse_next:
+                    eighth = wanted.astype(held8.dtype)
+                    held8[(hop + 1) % 2, :, span] = eighth
+                    owed[:, span] = (wanted - eighth.astype(jnp.float32)) * CARRY
+                elif hop + 1 < hops:
+                    held[(hop + 1) % 2, :, span] = wanted.astype(jnp.bfloat16)
                 if last:
                     part = value * value
                     total = part[:, :128]
@@ -164,7 +173,10 @@
 
     def account(s):
         scale = scale_row[...]
-        rms = jnp.sqrt(row_sums(squares[...]) * (1.0 / sites) * scale * scale + EPS)
+        power = row_sums(squares[...]) * (1.0 / sites)
+        if s == 0:
+            level_row[...] = LEVEL_LATER / jnp.sqrt(power + 1e-30)
+        rms = jnp.sqrt(power * scale * scale + EPS)
         scale_row[...] = scale / rms
         gained = jnp.log(rms)
         for slot in range(1 + len(log_dist)):
@@ -174,7 +186,7 @@
                 logs[slot] = logs[slot] + gained
 
     for s in range(STEPS):
-        advance(s, s * SPAN < COARSE)
+        advance(s)
         account(s)
         if s == STEPS - 2:
             for i in range(len(log_dist)):
@@ -230,6 +242,7 @@
             pltpu.VMEM((1 + ways, 8, rows), jnp.float32),
             pltpu.VMEM((ways, 8, rows), jnp.float32),
             pltpu.VMEM((8, rows), jnp.float32),
+            pltpu.VMEM((8, rows), jnp.float32),
             pltpu.SemaphoreType.DMA,
             pltpu.SemaphoreType.DMA((reach,)),
             pltpu.SemaphoreType.DMA((reach,)),

time: 27.1 us -> 24.6 us (0.908)
  Pallas kernels: 23.9 us -> 21.3 us
    pallas_call x1, Pallas kernels: 23.9 us -> 21.3 us  [shards(): pl.pallas_call(functools.partial(kernel, slices), out_shape=(jax.ShapeDty...]
where the time goes in v5:
time: 24.6 us; the launch traced here: 24.4 us
  Pallas kernels  21.3 us (87%)
  other arithmetic  1.35 us (5%)
  local copies, waits for them, and re-layouts  1.06 us (4%)
  between operations  0.64 us (3%)
    pallas_call x1, Pallas kernels, shards(): pl.pallas_call(functools.partial(kernel, slices), out_shape=(jax.ShapeDty...  21.3 us
    unnamed x1, local copies, waits for them, and re-layouts  1.06 us
    concatenate x1, other arithmetic, shards(): jnp.concatenate([neighbours.T, spins], axis=0)  0.75 us
    pallas_call x1, other arithmetic, shards(): pl.pallas_call(functools.partial(kernel, slices), out_shape=(jax.ShapeDty...  0.6 us

profile of v5, /device:TPU:0, one launch (start us, length us, event | category | flops | bytes accessed | tf_op | source)
XLA Modules:
  0.0 24.4 jit_solution(4589138387822458091)
XLA Ops:
  0.6 0.8 %pad_add_fusion.table = s32[5,1152]{1,0:T(8,128)S(1)} fusion(s32[1,1152]{1,0:T(1,128)} %param.3, s32[4,1152]{1,0:T(4,128)} %bitcast.1), kind=kLoop, calls=%fused_computation | loop fusion | flops 5760 | bytes 46080 | tf_op jit(solution)/shard_map/concatenate | solution.py:259
  1.4 21.3 %shard_map.50 = (f32[288,1152]{1,0:T(8,128)S(1)}, f32[1,288]{1,0:T(1,128)S(1)}) custom-call(s32[5,1152]{1,0:T(8,128)S(1)} %pad_add_fusion.table, f32[288,1152]{1,0:T(8,128)} %start_ref.1), custom_call_target="tpu_custom_call" | custom-call | flops 15288238080 | bytes 2654208 | tf_op jit(solution)/shard_map/pallas_call | solution.py:222
  22.7 0.6 %reduce = f32[288]{0:T(512)} reduce(f32[1,288]{1,0:T(1,128)S(1)} %get-tuple-element.5, f32[]{:T(128)} %constant.1), dimensions={0}, to_apply=%get-tuple-element.5.reduce_sub_computation | reduce | bytes 2308 | tf_op jit(solution)/shard_map/pallas_call | solution.py:222
  23.3 1.1 %copy.6 = f32[288,1152]{1,0:T(8,128)} copy(f32[288,1152]{1,0:T(8,128)S(1)} %get-tuple-element.8) | data formatting | bytes 2654208

commit v6 on v5

--- a/solution.py
+++ b/solution.py
@@ -120,7 +120,7 @@
         now[:, lo:lo + 128] = value
         eighth = value.astype(held8.dtype)
         held8[0, :, lo:lo + 128] = eighth
-        owed[:, lo:lo + 128] = (value - eighth.astype(jnp.float32)) * CARRY
+        owed[:, lo:lo + 128] = ((value - eighth.astype(jnp.float32)) * CARRY).astype(owed.dtype)
 
     for copy in sends:
         copy.wait()
@@ -151,7 +151,7 @@
                 else:
                     moved = jnp.dot(held[hop % 2], rest[:, span], preferred_element_type=jnp.float32)
                 value = (now[:, span] + moved) * factor[:, span]
-                debt = owed[:, span] if coarse else None
+                debt = owed[:, span].astype(jnp.float32) if coarse else None
                 if rescale:
                     wide = jnp.concatenate([column] * (width // 128), axis=1)
                     value = value * wide
@@ -161,7 +161,7 @@
                 if coarse_next:
                     eighth = wanted.astype(held8.dtype)
                     held8[(hop + 1) % 2, :, span] = eighth
-                    owed[:, span] = (wanted - eighth.astype(jnp.float32)) * CARRY
+                    owed[:, span] = ((wanted - eighth.astype(jnp.float32)) * CARRY).astype(owed.dtype)
                 elif hop + 1 < hops:
                     held[(hop + 1) % 2, :, span] = wanted.astype(jnp.bfloat16)
                 if last:
@@ -237,7 +237,7 @@
             pltpu.VMEM((rows, sites), jnp.float32),
             pltpu.VMEM((2, rows, sites), jnp.bfloat16),
             pltpu.VMEM((2, rows, sites), jnp.float8_e4m3fn),
-            pltpu.VMEM((rows, sites), jnp.float32),
+            pltpu.VMEM((rows, sites), jnp.bfloat16),
             pltpu.VMEM((rows, 128), jnp.float32),
             pltpu.VMEM((1 + ways, 8, rows), jnp.float32),
             pltpu.VMEM((ways, 8, rows), jnp.float32),

time: 24.6 us -> 24.7 us (level)
  no operation moved by 1% of the time
where the time goes in v6:
time: 24.7 us; the launch traced here: 24.5 us
  Pallas kernels  21.5 us (87%)
  other arithmetic  1.35 us (5%)
  local copies, waits for them, and re-layouts  1.06 us (4%)
  between operations  0.64 us (3%)
    pallas_call x1, Pallas kernels, shards(): pl.pallas_call(functools.partial(kernel, slices), out_shape=(jax.ShapeDty...  21.5 us
    unnamed x1, local copies, waits for them, and re-layouts  1.06 us
    concatenate x1, other arithmetic, shards(): jnp.concatenate([neighbours.T, spins], axis=0)  0.75 us
    pallas_call x1, other arithmetic, shards(): pl.pallas_call(functools.partial(kernel, slices), out_shape=(jax.ShapeDty...  0.6 us

profile of v6, /device:TPU:0, one launch (start us, length us, event | category | flops | bytes accessed | tf_op | source)
XLA Modules:
  0.0 24.5 jit_solution(5379841675821424884)
XLA Ops:
  0.6 0.8 %pad_add_fusion.table = s32[5,1152]{1,0:T(8,128)S(1)} fusion(s32[1,1152]{1,0:T(1,128)} %param.3, s32[4,1152]{1,0:T(4,128)} %bitcast.1), kind=kLoop, calls=%fused_computation | loop fusion | flops 5760 | bytes 46080 | tf_op jit(solution)/shard_map/concatenate | solution.py:259
  1.4 21.5 %shard_map.50 = (f32[288,1152]{1,0:T(8,128)S(1)}, f32[1,288]{1,0:T(1,128)S(1)}) custom-call(s32[5,1152]{1,0:T(8,128)S(1)} %pad_add_fusion.table, f32[288,1152]{1,0:T(8,128)} %start_ref.1), custom_call_target="tpu_custom_call" | custom-call | flops 15288238080 | bytes 2654208 | tf_op jit(solution)/shard_map/pallas_call | solution.py:222
  22.8 0.6 %reduce = f32[288]{0:T(512)} reduce(f32[1,288]{1,0:T(1,128)S(1)} %get-tuple-element.5, f32[]{:T(128)} %constant.1), dimensions={0}, to_apply=%get-tuple-element.5.reduce_sub_computation | reduce | bytes 2308 | tf_op jit(solution)/shard_map/pallas_call | solution.py:222
  23.4 1.1 %copy.6 = f32[288,1152]{1,0:T(8,128)} copy(f32[288,1152]{1,0:T(8,128)S(1)} %get-tuple-element.8) | data formatting | bytes 2654208
